TPU v7x, 256 devices: a whole 4x4x8 slice. The times are simulated.
256 devices in a mesh: pair: 64 (over z, x, core), ri: 4 (over y).
Axes of the slice: x: 4, y: 4, z: 8, core: 2. Of those that a mesh axis runs over, the one named last changes fastest.
Arguments:
- tensor: bfloat16 [64, 3, 192, 128, 128], P('pair', None, 'ri'), may hold values from -0.875 to 0.875
- live: int32 [64, 3], replicated, may hold values 0 or 1
- sizes: int32 [64], replicated, may hold values from 64 to 128
- occ_density: bfloat16 [64, 3, 128, 128], P('pair', None, 'ri'), may hold values from -0.2066757 to 0.2066757, as said below
- vir_density: bfloat16 [64, 3, 128, 128], P('pair', None, 'ri'), may hold values from -0.2066757 to 0.2066757, as said below
Outputs:
- chi: float32 [64, 3, 192, 192], P('pair', None, None, 'ri')
Inputs may be any that keep to these rules, and one draw needn't show every extreme that they name: `occ_density`: the blocks form a symmetric matrix: block (a, a+k) is the transpose of block (a+k, a), cluster indices modulo 64. `vir_density`: the blocks form a symmetric matrix: block (a, a+k) is the transpose of block (a+k, a), cluster indices modulo 64.
All inputs are finite; a program needn't handle non-finite values.
Results may differ from a plain program's by a relative error of at most 0.004.
Values may be sent and summed in bfloat16 or wider, within the bound.
A program may use at most 192 MiB of HBM per device.

v0:
```python
from functools import partial

import jax
import jax.numpy as jnp
from jax import lax
from jax.sharding import PartitionSpec as P


def from_behind(array, axis, by):
    length = lax.axis_size(axis)
    return lax.ppermute(array, axis, [(i, (i + by) % length) for i in range(length)])


def block_product(tensor_rows, panel):
    depth_count, row_count, inner_count = tensor_rows.shape
    flat_rows = jnp.dot(
        tensor_rows.reshape(depth_count * row_count, inner_count),
        panel,
        preferred_element_type=jnp.float32,
    )
    return flat_rows.reshape(depth_count, row_count, panel.shape[1])


def half_products(source_rows, panels, t, tile_shape):
    running = jnp.zeros(tile_shape, jnp.float32)
    for s in (-1, 0, 1):
        if abs(t - s) <= 1:
            maker = partial(block_product, source_rows[s + 1], panels[s][t - s + 1])
            running = running + maker()
    return running.astype(jnp.bfloat16)


def per_device(tensor, live, sizes, occ_density, vir_density):
    occ_full, vir_full = (
        lax.all_gather(occ_density, "ri", axis=2, tiled=True),
        lax.all_gather(vir_density, "ri", axis=2, tiled=True),
    )
    occ_row = occ_full[0]
    vir_row = vir_full[0]
    basis_width = tensor.shape[-1]
    ri_share = tensor.shape[2]
    ri_count = lax.axis_size("ri")
    cluster_count = lax.axis_size("pair")
    cluster_index = lax.axis_index("pair")
    lane_index = jnp.arange(basis_width, dtype=jnp.int32)
    cluster_ids = jnp.arange(cluster_count, dtype=jnp.int32)
    offsets = jnp.arange(-1, 2, dtype=jnp.int32)
    chosen = cluster_ids[None, :] == jnp.mod(cluster_index + offsets, cluster_count)[:, None]
    nbr_sizes = jnp.sum(jnp.where(chosen, sizes[None, :], 0), axis=1)
    picked = cluster_ids == jnp.mod(cluster_index, cluster_count)
    own_flags = jnp.sum(jnp.where(picked[:, None], live, 0), axis=0)
    keep_mask = (
        (own_flags[:, None, None] > 0)
        & (lane_index[None, :, None] < nbr_sizes[1])
        & (lane_index[None, None, :] < nbr_sizes[:, None, None])
    )
    masked = tensor[0] * keep_mask[:, None, :, :].astype(tensor.dtype)
    own_regrouped = lax.all_to_all(masked, "ri", split_axis=2, concat_axis=1, tiled=True)
    tile_shape = (ri_share, basis_width, basis_width)
    near_list = []
    panels = {0: vir_row}
    for s in (1, -1):
        panels[s] = from_behind(vir_row, "pair", -s)
    halves = {}
    for t in range(-2, 3):
        halves[t] = half_products(masked, panels, t, tile_shape)
    arrived = {}
    for g in (-1, 0, 1):
        outgoing = jnp.stack(
            [
                jnp.einsum(
                    "mn,pms->pns", occ_row[1 - g], halves[u - g], preferred_element_type=jnp.float32
                ).astype(jnp.bfloat16)
                for u in (-1, 0, 1)
            ]
        )
        if g == 0:
            arrived[g] = outgoing
        else:
            arrived[g] = from_behind(outgoing, "pair", -g)
    near_list = [arrived[g] for g in (-1, 0, 1)]
    near_all = jnp.stack(near_list).reshape(9, ri_share, basis_width, basis_width)
    regrouped = lax.all_to_all(near_all, "ri", split_axis=2, concat_axis=1, tiled=True)
    ri_whole = regrouped.shape[1]
    near_flat = regrouped.reshape(3, 3, ri_whole, -1)
    own_flat = own_regrouped.reshape(3, ri_whole, -1)
    polar_terms = jnp.einsum(
        "gupk,uqk->gpq", near_flat, own_flat, preferred_element_type=jnp.float32
    )
    column_share = ri_whole // ri_count
    summed = lax.psum(polar_terms, "ri")
    result = lax.dynamic_slice_in_dim(summed, lax.axis_index("ri") * column_share, column_share, 2)
    return result[None]


def solution(mesh):
    in_specs = (
        P("pair", None, "ri", None, None),
        P(),
        P(),
        P("pair", None, "ri", None),
        P("pair", None, "ri", None),
    )
    out_specs = P("pair", None, None, "ri")
    return jax.shard_map(
        per_device, mesh=mesh, in_specs=in_specs, out_specs=out_specs, check_vma=False
    )
```

profile of v0, /device:TPU:8, one launch (start us, length us, event | category | flops | bytes accessed | tf_op | source)
XLA Modules:
  0.0 415.5 jit_solution(15411814747586273254)
XLA Ops:
  6.5 12.4 %all_gather.6 = bf16[1,3,128,128]{3,2,1,0:T(8,128)(2,1)S(1)} all-gather(bf16[1,3,32,128]{3,2,1,0:T(8,128)(2,1)} %param.9), channel_id=1, replica_groups=mesh['pair'=64,'ri'=4] {'ri'}, dimensions={2}, use_global_device_ids=true | all-gather | bytes 122880 | tf_op jit(solution)/shard_map/all_gather | solution.py:36
  18.9 4.6 %collective-permute-start.1 = (bf16[3,128,128]{2,1,0:T(8,128)(2,1)S(1)}, bf16[3,128,128]{2,1,0:T(8,128)(2,1)S(1)}, u32[]{:S(2)}, u32[]{:S(2)}) collective-permute-start(bf16[3,128,128]{2,1,0:T(8,128)(2,1)S(1)} %bitcast.155), channel_id=1, source_target_pairs={{0,252},{4,0},{8,4},{12,8},{16,12},{20,16},{24,20},{28,24},{32,28}... | collective-permute-start | bytes 294920 | tf_op jit(solution)/shard_map/ppermute | solution.py:11
  23.5 0.8 select_reduce_fusion
  24.4 0.6 slice.66
  25.0 0.6 iota_compare_fusion.2
  25.6 0.8 select_reduce_fusion.1
  26.4 0.1 iota_compare_fusion
  26.5 0.1 and_convert_fusion
  26.6 2.7 bitcast_multiply_fusion
  29.3 0.6 fusion.11
  29.8 0.6 fusion.10
  30.4 0.5 fusion.12
  31.0 0.2 copy-done.4
  31.2 11.9 %all_gather.7 = bf16[1,3,128,128]{3,2,1,0:T(8,128)(2,1)S(1)} all-gather(bf16[1,3,32,128]{3,2,1,0:T(8,128)(2,1)S(1)} %copy-done.4), channel_id=1, replica_groups=mesh['pair'=64,'ri'=4] {'ri'}, dimensions={2}, use_global_device_ids=true | all-gather | bytes 122880 | tf_op jit(solution)/shard_map/all_gather | solution.py:35
  43.1 0.6 fusion.9
  43.7 0.6 add_convert_fusion.2
  44.3 1.8 fusion.8
  46.1 1.8 fusion
  47.8 0.5 add_convert_fusion.1
  48.4 1.8 fusion.1
  50.2 0.5 add_convert_fusion
  50.8 1.1 copy-done.2
  51.9 1.8 fusion.7
  53.7 3.7 fusion.2
  57.4 5.0 %pad_maximum_fusion.1 = bf16[3,48,128,128]{2,3,1,0:T(8,128)(2,1)} fusion(bf16[1,48,128,128]{2,3,1,0:T(8,128)(2,1)} %fusion.2, bf16[1,48,128,128]{2,3,1,0:T(8,128)(2,1)} %fusion.1, bf16[1,48,128,128]{2,3,1,0:T(8,128)(2,1)} %fusion), kind=kLoop, calls=%fused_computation.1 | loop fusion | flops 4718592 | bytes 9437184 | tf_op jit(solution)/shard_map/stack | solution.py:69
  62.4 3.8 fusion.6
  66.2 5.1 %pad_maximum_fusion.2 = bf16[3,48,128,128]{2,3,1,0:T(8,128)(2,1)} fusion(bf16[1,48,128,128]{2,3,1,0:T(8,128)(2,1)} %fusion.8, bf16[1,48,128,128]{2,3,1,0:T(8,128)(2,1)} %fusion.7, bf16[1,48,128,128]{2,3,1,0:T(8,128)(2,1)} %fusion.6), kind=kLoop, calls=%fused_computation.3 | loop fusion | flops 4718592 | bytes 9437184 | tf_op jit(solution)/shard_map/stack | solution.py:69
  71.4 5.1 %collective-permute-start.3 = (bf16[3,48,128,128]{2,3,1,0:T(8,128)(2,1)}, bf16[3,48,128,128]{2,3,1,0:T(8,128)(2,1)}, u32[]{:S(2)}, u32[]{:S(2)}) collective-permute-start(bf16[3,48,128,128]{2,3,1,0:T(8,128)(2,1)} %pad_maximum_fusion.2), channel_id=1, source_target_pairs={{0,252},{4,0},{8,4},{12,8},{16,12},{20,16},{24,20},{28,24},{32,28}... | collective-permute-start | bytes 14155784 | tf_op jit(solution)/shard_map/ppermute | solution.py:11
  76.4 5.3 %copy.51 = bf16[3,48,128,128]{3,1,0,2:T(8,128)(2,1)} copy(bf16[3,48,128,128]{3,2,1,0:T(8,128)(2,1)S(1)} %bitcast.152) | data formatting | bytes 9437184 | tf_op jit(solution)/shard_map/mul | solution.py:57
  81.7 5.8 %all-to-all-start.1 = ((bf16[3,48,128,128]{3,1,0,2:T(8,128)(2,1)}), bf16[3,48,128,128]{3,1,0,2:T(8,128)(2,1)}, u32[]{:S(2)}, u32[]{:S(2)}) async-start(bf16[3,48,128,128]{3,1,0,2:T(8,128)(2,1)} %copy.51), calls=%async_computation.1 | async-start | bytes 9437184 | tf_op jit(solution)/shard_map/all_to_all | solution.py:58
  87.4 2.1 fusion.5
  89.6 0.6 fusion.3
  90.2 0.6 fusion.4
  90.8 0.6 maximum_bitcast_fusion
  91.4 28.2 %collective-permute-done.2 = bf16[3,48,128,128]{2,3,1,0:T(8,128)(2,1)} collective-permute-done((bf16[3,48,128,128]{2,3,1,0:T(8,128)(2,1)}, bf16[3,48,128,128]{2,3,1,0:T(8,128)(2,1)}, u32[]{:S(2)}, u32[]{:S(2)}) %collective-permute-start.2) | collective-permute-done | bytes 4718624 | tf_op jit(solution)/shard_map/ppermute | solution.py:11
  119.6 8.7 %collective-permute-done.3 = bf16[3,48,128,128]{2,3,1,0:T(8,128)(2,1)} collective-permute-done((bf16[3,48,128,128]{2,3,1,0:T(8,128)(2,1)}, bf16[3,48,128,128]{2,3,1,0:T(8,128)(2,1)}, u32[]{:S(2)}, u32[]{:S(2)}) %collective-permute-start.3) | collective-permute-done | bytes 4718624 | tf_op jit(solution)/shard_map/ppermute | solution.py:11
  128.4 10.7 %pad_maximum_fusion = bf16[3,3,48,128,128]{3,4,2,1,0:T(8,128)(2,1)} fusion(bf16[1,3,48,128,128]{3,4,2,1,0:T(8,128)(2,1)} %bitcast.53, bf16[1,3,48,128,128]{3,4,2,1,0:T(8,128)(2,1)S(1)} %maximum_bitcast_fusion, bf16[1,3,48,128,128]{3,4,2,1,0:T(8,128)(2,1)} %bitcast.27), kind=kLoop, calls=%fused_computation | loop fusion | flops 14155776 | bytes 28311552 | tf_op jit(solution)/shard_map/stack | solution.py:82
  139.0 18.3 %copy.48 = bf16[9,48,128,128]{3,1,0,2:T(8,128)(2,1)} copy(bf16[9,48,128,128]{2,3,1,0:T(8,128)(2,1)} %bitcast.153) | data formatting | bytes 28311552 | tf_op jit(solution)/shard_map/reshape | solution.py:82
  157.4 7.3 %all-to-all-start = ((bf16[9,48,128,128]{3,1,0,2:T(8,128)(2,1)}), bf16[9,48,128,128]{3,1,0,2:T(8,128)(2,1)}, u32[]{:S(2)}, u32[]{:S(2)}) async-start(bf16[9,48,128,128]{3,1,0,2:T(8,128)(2,1)} %copy.48), calls=%async_computation | async-start | bytes 28311552 | tf_op jit(solution)/shard_map/all_to_all | solution.py:83
  164.7 5.8 %copy.65 = bf16[3,48,4,32,128]{4,3,1,2,0:T(8,128)(2,1)} copy(bf16[3,48,4,32,128]{4,1,0,3,2:T(8,128)(2,1)} %bitcast.58) | data formatting | bytes 9437184 | tf_op jit(solution)/shard_map/all_to_all | solution.py:58
  170.5 8.2 %reshape.151 = bf16[3,192,4096,1]{2,1,0,3:T(8,128)(2,1)} reshape(bf16[3,4,48,32,128]{4,3,2,1,0:T(8,128)(2,1)} %bitcast.154) | data formatting | bytes 9437184 | tf_op jit(solution)/shard_map/reshape | solution.py:86
  178.7 135.2 %all-to-all-done = bf16[9,48,128,128]{3,1,0,2:T(8,128)(2,1)} async-done(((bf16[9,48,128,128]{3,1,0,2:T(8,128)(2,1)}), bf16[9,48,128,128]{3,1,0,2:T(8,128)(2,1)}, u32[]{:S(2)}, u32[]{:S(2)}) %all-to-all-start) | async-done | bytes 14155808 | tf_op jit(solution)/shard_map/all_to_all | solution.py:83
  313.9 12.5 %copy.50 = bf16[9,4,48,32,128]{4,3,2,1,0:T(8,128)(2,1)} copy(bf16[9,4,48,32,128]{4,2,0,3,1:T(8,128)(2,1)} %bitcast.57) | data formatting | bytes 28311552 | tf_op jit(solution)/shard_map/all_to_all | solution.py:83
  326.4 21.6 %reshape.137 = bf16[3,3,192,4096]{3,2,1,0:T(8,128)(2,1)} reshape(bf16[9,4,48,32,128]{4,3,2,1,0:T(8,128)(2,1)} %copy.50) | data formatting | bytes 28311552 | tf_op jit(solution)/shard_map/reshape | solution.py:85
  348.0 11.0 %convolution_bitcast_fusion = f32[3,192,192]{1,2,0:T(8,128)} fusion(bf16[3,3,192,4096]{3,2,1,0:T(8,128)(2,1)} %reshape.137, bf16[3,192,4096,1]{2,1,0,3:T(8,128)(2,1)} %reshape.151), kind=kOutput, calls=%fused_computation.32 | convolution fusion | flops 2717908992 | bytes 19316736 | tf_op jit(solution)/shard_map/gupk,uqk->gpq/dot_general | solution.py:87
  359.0 0.0 all-reduce.2.cloned.1.call-update
  359.0 48.0 %all-reduce.2.cloned.1.call-done = f32[3,192,192]{1,2,0:T(8,128)} async-done(((f32[3,192,192]{1,2,0:T(8,128)}), f32[3,192,192]{1,2,0:T(8,128)}) %all-reduce.2.cloned.1.call-update) | async-done | bytes 442384 | tf_op jit(solution)/shard_map/psum | solution.py:91
  407.1 1.6 dynamic-slice_bitcast_fusion
  (22 shorter events, 0.1 us)
Async XLA Ops:
  18.9 24.8 %collective-permute-start.1 = (bf16[3,128,128]{2,1,0:T(8,128)(2,1)S(1)}, bf16[3,128,128]{2,1,0:T(8,128)(2,1)S(1)}, u32[]{:S(2)}, u32[]{:S(2)}) collective-permute-start(bf16[3,128,128]{2,1,0:T(8,128)(2,1)S(1)} %bitcast.155), channel_id=1, source_target_pairs={{0,252},{4,0},{8,4},{12,8},{16,12},{20,16},{24,20},{28,24},{32,28}... | collective-permute-start | bytes 294920 | tf_op jit(solution)/shard_map/ppermute | solution.py:11
  23.5 19.6 %collective-permute-start = (bf16[3,128,128]{2,1,0:T(8,128)(2,1)S(1)}, bf16[3,128,128]{2,1,0:T(8,128)(2,1)S(1)}, u32[]{:S(2)}, u32[]{:S(2)}) collective-permute-start(bf16[3,128,128]{2,1,0:T(8,128)(2,1)S(1)} %bitcast.156), channel_id=1, source_target_pairs={{0,4},{4,8},{8,12},{12,16},{16,20},{20,24},{24,28},{28,32},{32,36}... | collective-permute-start | bytes 294920 | tf_op jit(solution)/shard_map/ppermute | solution.py:11
  29.3 20.9 %copy-start = (bf16[3,48,128,128]{3,2,1,0:T(8,128)(2,1)}, bf16[3,48,128,128]{3,2,1,0:T(8,128)(2,1)S(1)}, u32[]{:S(2)}) copy-start(bf16[3,48,128,128]{3,2,1,0:T(8,128)(2,1)S(1)} %bitcast_multiply_fusion) | copy-start | bytes 14155780
  30.4 0.8 copy-start.4
  48.4 2.3 copy-start.1
  50.8 1.2 copy-start.2
  62.4 57.2 %collective-permute-start.2 = (bf16[3,48,128,128]{2,3,1,0:T(8,128)(2,1)}, bf16[3,48,128,128]{2,3,1,0:T(8,128)(2,1)}, u32[]{:S(2)}, u32[]{:S(2)}) collective-permute-start(bf16[3,48,128,128]{2,3,1,0:T(8,128)(2,1)} %pad_maximum_fusion.1), channel_id=1, source_target_pairs={{0,4},{4,8},{8,12},{12,16},{16,20},{20,24},{24,28},{28,32},{32,36}... | collective-permute-start | bytes 14155784 | tf_op jit(solution)/shard_map/ppermute | solution.py:11
  62.4 14.0 %slice-start = ((s8[4718592]{0:T(1024)(128)(4,1)}), s8[524288]{0:T(1024)(128)(4,1)S(1)}, s32[]{:S(2)}) async-start(s8[4718592]{0:T(1024)(128)(4,1)} %bitcast.151), calls=%async_computation.3 | async-start | bytes 1048576
  66.2 10.2 %slice-start.1 = ((s8[4718592]{0:T(1024)(128)(4,1)}), s8[4194304]{0:T(1024)(128)(4,1)S(1)}, s32[]{:S(2)}) async-start(s8[4718592]{0:T(1024)(128)(4,1)} %bitcast.151), calls=%async_computation.4 | async-start | bytes 8388608
  71.4 57.0 %collective-permute-start.3 = (bf16[3,48,128,128]{2,3,1,0:T(8,128)(2,1)}, bf16[3,48,128,128]{2,3,1,0:T(8,128)(2,1)}, u32[]{:S(2)}, u32[]{:S(2)}) collective-permute-start(bf16[3,48,128,128]{2,3,1,0:T(8,128)(2,1)} %pad_maximum_fusion.2), channel_id=1, source_target_pairs={{0,252},{4,0},{8,4},{12,8},{16,12},{20,16},{24,20},{28,24},{32,28}... | collective-permute-start | bytes 14155784 | tf_op jit(solution)/shard_map/ppermute | solution.py:11
  81.7 75.7 %all-to-all-start.1 = ((bf16[3,48,128,128]{3,1,0,2:T(8,128)(2,1)}), bf16[3,48,128,128]{3,1,0,2:T(8,128)(2,1)}, u32[]{:S(2)}, u32[]{:S(2)}) async-start(bf16[3,48,128,128]{3,1,0,2:T(8,128)(2,1)} %copy.51), calls=%async_computation.1 | async-start | bytes 9437184 | tf_op jit(solution)/shard_map/all_to_all | solution.py:58
  87.4 2.1 copy-start.3
  157.4 156.5 %all-to-all-start = ((bf16[9,48,128,128]{3,1,0,2:T(8,128)(2,1)}), bf16[9,48,128,128]{3,1,0,2:T(8,128)(2,1)}, u32[]{:S(2)}, u32[]{:S(2)}) async-start(bf16[9,48,128,128]{3,1,0,2:T(8,128)(2,1)} %copy.48), calls=%async_computation | async-start | bytes 28311552 | tf_op jit(solution)/shard_map/all_to_all | solution.py:83
  164.7 242.3 %all-reduce.2.cloned.1.call-start = ((), (), s32[]{:S(2)}) async-start(), calls=%async_computation.2 | async-start | bytes 1179648 | tf_op jit(solution)/shard_map/psum | solution.py:91
Sparse Core Ops, SparseCore 0:
  359.1 47.8 all-reduce.1
where the time goes:
time: 418 us; the launch traced here: 415 us
  waiting for transfers between devices  220 us (53%)
  local copies, waits for them, and re-layouts  75.2 us (18%)
  matrix products  32.9 us (8%)
  other arithmetic  26.6 us (6%)
  blocking collectives  24.3 us (6%)
  starting transfers between devices  22.8 us (5%)
  between operations  13.6 us (3%)
    all_to_all x1, waiting for transfers between devices, per_device(): lax.all_to_all(near_all, 'ri', split_axis=2, concat_axis=1, tiled=True)  135 us
    psum x1, waiting for transfers between devices, per_device(): summed = lax.psum(polar_terms, 'ri')  48 us
    ppermute x4, waiting for transfers between devices, from_behind(): lax.ppermute(array, axis, [(i, (i + by) % length) for i in range(length)])  37 us
    reshape x1, local copies, waits for them, and re-layouts, per_device(): near_flat = regrouped.reshape(3, 3, ri_whole, -1)  21.6 us
    reshape x1, local copies, waits for them, and re-layouts, per_device(): jnp.stack(near_list).reshape(9, ri_share, basis_width, basis_width)  18.3 us
    dot_general x9, matrix products, per_device(): jnp.einsum('mn,pms->pns', occ_row[1 - g], halves[u - g], preferred_elemen...  18 us
    all_to_all x1, local copies, waits for them, and re-layouts, per_device(): lax.all_to_all(near_all, 'ri', split_axis=2, concat_axis=1, tiled=True)  12.5 us
    all_gather x1, blocking collectives, per_device(): lax.all_gather(vir_density, 'ri', axis=2, tiled=True)  12.4 us
  transfers between devices with their start and end apart: 7, of which 4 were waited for; matrix products, arithmetic and copies ran while one was open for 17% of the time, Pallas kernels for 0%

commit v1 on v0

v1 whole, which is shorter than its diff:
```python
import functools

import jax
import jax.numpy as jnp
from jax import lax
from jax.experimental import pallas as pl
from jax.experimental.pallas import tpu as pltpu
from jax.sharding import PartitionSpec as P

MESH = pl.DeviceIdType.MESH
BF = jnp.bfloat16
F32 = jnp.float32
NT = (((1,), (1,)), ((), ()))
MC = 32
LAG = 2


def kernel(
    ncl, nri,
    ten, live, sizes, occ, vir,
    out,
    nat, fnat, own_t, up_t, c1a, c1b, cmb,
    z0, zp, zm, f0, fp, zn, perm, vmat, omat, occ_f, vir_f, acc, rin, rsend,
    s_nat, r_nat, l_nat, s_up, r_up, s_c1a, r_c1a, s_c1b, r_c1b, s_cmb, r_cmb,
    s_occ, r_occ, s_vir, r_vir, l_den, s_res, r_res,
):
    S = ten.shape[2]
    B = ten.shape[3]
    DR = occ.shape[2]
    NQ = S // 16
    NMC = B // MC
    NK = 3 * NMC
    c = lax.axis_index("pair")
    y = lax.axis_index("ri")

    def cl(d):
        return lax.rem(c + (d + ncl), ncl)

    def rw(d):
        return lax.rem(y + (d + nri), nri)

    def remote(src, dst, ss, rs, dc, dy):
        return pltpu.make_async_remote_copy(
            src_ref=src, dst_ref=dst, send_sem=ss, recv_sem=rs,
            device_id=(cl(dc), rw(dy)), device_id_type=MESH,
        )

    barrier = pltpu.get_barrier_semaphore()
    others = [(dc, dy) for dc in (-1, 0, 1) for dy in range(nri) if (dc, dy) != (0, 0)]
    for dc, dy in others:
        pl.semaphore_signal(barrier, inc=1, device_id=(cl(dc), rw(dy)), device_id_type=MESH)

    nat_copies = [
        pltpu.make_async_copy(ten.at[0, s], nat.at[s], l_nat.at[s]) for s in range(3)
    ]
    for cp in nat_copies:
        cp.start()
    my_rows = pl.ds(pl.multiple_of(y * DR, DR), DR)
    den_copies = [
        pltpu.make_async_copy(occ.at[0], occ_f.at[:, my_rows], l_den.at[0]),
        pltpu.make_async_copy(vir.at[0], vir_f.at[1, :, my_rows], l_den.at[1]),
    ]
    for cp in den_copies:
        cp.start()
    row = lax.broadcasted_iota(jnp.int32, (256, 256), 0)
    col = lax.broadcasted_iota(jnp.int32, (256, 256), 1)
    perm[...] = jnp.where(
        (row // 16 == col % 16) & (row % 16 == col // 16), 1.0, 0.0
    ).astype(BF)
    for r in range(acc.shape[0]):
        acc[r] = jnp.zeros(acc.shape[1:], F32)
    pl.semaphore_wait(barrier, len(others))

    occ_sends, vir_sends = [], []
    for dy in range(1, nri):
        occ_sends.append(
            remote(occ.at[0], occ_f.at[:, my_rows], s_occ.at[dy - 1], r_occ.at[dy - 1], 0, dy)
        )
    for i, (dc, dy) in enumerate(others):
        vir_sends.append(
            remote(vir.at[0], vir_f.at[1 - dc, :, my_rows], s_vir.at[i], r_vir.at[i], dc, dy)
        )
    for cp in occ_sends + vir_sends:
        cp.start()

    nat_sends = []
    for j in range(NQ):
        q = pl.ds(16 * j, 16)
        nat_sends.append(
            remote(ten.at[0, :, q], fnat.at[:, q], s_nat.at[j], r_nat.at[j], 0, 1)
        )
    for cp in nat_sends:
        cp.start()

    def part(k):
        return lax.div(k, NMC), pl.ds(pl.multiple_of(lax.rem(k, NMC) * MC, MC), MC)

    def up_send(k):
        s, m = part(k)
        return remote(own_t.at[s, m], up_t.at[s, m], s_up.at[k], r_up.at[k], 0, -1)

    def c1a_send(k):
        s, m = part(k)
        return remote(own_t.at[s, m], c1a.at[s, m], s_c1a.at[k], r_c1a.at[k], -1, 0)

    def c1b_send(k):
        s, m = part(k)
        return remote(up_t.at[s, m], c1b.at[s, m], s_c1b.at[k], r_c1b.at[k], -1, 0)

    def cmb_send(k):
        s, m = part(k)
        return remote(up_t.at[s, m], cmb.at[s, m], s_cmb.at[k], r_cmb.at[k], 1, 0)

    for s in range(3):
        nat_copies[s].wait()

        @pl.loop(0, NMC)
        def _(mc, s=s):
            for mb in range(MC // 16):
                m0 = pl.multiple_of(mc * MC + mb * 16, 16)
                for j in range(NQ):
                    x = nat[s, pl.ds(16 * j, 16), pl.ds(m0, 16), :].reshape(256, B)
                    t = jnp.dot(perm[...], x, preferred_element_type=F32).astype(BF)
                    own_t[s, pl.ds(m0, 16), pl.ds(16 * j, 16), :] = t.reshape(16, 16, B)
            k = s * NMC + mc
            up_send(k).start()
            c1a_send(k).start()

    for cp in den_copies:
        cp.wait()
    for cp in occ_sends + vir_sends:
        cp.wait_recv()
    size = {d: sizes[cl(d)] for d in range(-2, 3)}
    ri_ = lax.broadcasted_iota(jnp.int32, (B, B), 0)
    ci_ = lax.broadcasted_iota(jnp.int32, (B, B), 1)
    for u in (-1, 0, 1):
        on = live[c, u + 1].astype(F32)
        for t in (u - 1, u, u + 1):
            keep = jnp.where((ri_ < size[u]) & (ci_ < size[t]), on, 0.0)
            v = vir_f[u + 1, t - u + 1].astype(F32) * keep
            vmat[pl.ds((u + 1) * B, B), pl.ds((t + 2) * B, B)] = v.astype(BF)
    zero = jnp.zeros((B, B), BF)
    for u in (-1, 0, 1):
        for t in range(-2, 3):
            if abs(t - u) > 1:
                vmat[pl.ds((u + 1) * B, B), pl.ds((t + 2) * B, B)] = zero
    for g in (-1, 0, 1):
        o = occ_f[g + 1].astype(F32)
        o = jnp.where((ri_ < size[0]) & (ci_ < size[g]), o, 0.0)
        omat[g + 1] = o.T.astype(BF)

    def transform(src, q0, dests):
        @pl.loop(0, 8)
        def _(i):
            qs = [q0 + 2 * i, q0 + 2 * i + 1]
            x = jnp.concatenate(
                [jnp.concatenate([src[u, q] for u in range(3)], axis=1) for q in qs], axis=0
            )
            lo = jnp.dot(
                x[:, : 2 * B], vmat[pl.ds(0, 2 * B), pl.ds(0, 2 * B)],
                preferred_element_type=F32,
            ).astype(BF)
            mid = jnp.dot(
                x, vmat[:, pl.ds(2 * B, B)], preferred_element_type=F32
            ).astype(BF)
            hi = jnp.dot(
                x[:, B:], vmat[pl.ds(B, 2 * B), pl.ds(3 * B, 2 * B)],
                preferred_element_type=F32,
            ).astype(BF)
            yy = jnp.concatenate([lo, mid, hi], axis=1)
            for n in range(2):
                rows = yy[n * B : (n + 1) * B]
                for slot, (g, _dst) in enumerate(dests):
                    zn[slot, 2 * i + n] = jnp.dot(
                        omat[g + 1], rows[:, (g + 1) * B : (g + 4) * B],
                        preferred_element_type=F32,
                    ).astype(BF)

        @pl.loop(0, B // 16)
        def _(mb):
            m0 = pl.multiple_of(mb * 16, 16)
            for slot, (_g, dst) in enumerate(dests):
                x = zn[slot, :, pl.ds(m0, 16), :].reshape(256, 3 * B)
                t = jnp.dot(perm[...], x, preferred_element_type=F32).astype(BF)
                for s in range(3):
                    dst[s, pl.ds(m0, 16), pl.ds(q0, 16), :] = t[
                        :, s * B : (s + 1) * B
                    ].reshape(16, 16, B)

    @pl.loop(0, NQ)
    def _(j):
        transform(nat, pl.multiple_of(16 * j, 16), [(-1, zm), (0, z0), (1, zp)])

    def gram(r, left, right, dc, k):
        s, _ = part(k)
        m0 = lax.rem(k, NMC) * MC
        total = jnp.zeros((S, S), F32)
        for i in range(MC // 2):
            a = jnp.concatenate([left[s, m0 + 2 * i], left[s, m0 + 2 * i + 1]], axis=1)
            b = jnp.concatenate([right[s, m0 + 2 * i], right[s, m0 + 2 * i + 1]], axis=1)
            total += lax.dot_general(a, b, NT, preferred_element_type=F32)
        acc[r] += total * live[cl(dc), s].astype(F32)

    def late(k):
        c1b_send(k).wait_recv()
        gram(4, c1b, zp, 1, k)
        cmb_send(k).wait_recv()
        gram(6, cmb, zm, -1, k)

    cpj = NK // NQ

    @pl.loop(0, NQ)
    def _(j):
        @pl.loop(0, cpj)
        def _(kk):
            k = j * cpj + kk
            up_send(k).wait_recv()
            c1b_send(k).start()
            cmb_send(k).start()
            gram(0, own_t, z0, 0, k)
            gram(1, up_t, z0, 0, k)
            c1a_send(k).wait_recv()
            gram(3, c1a, zp, 1, k)

            @pl.when(k >= LAG)
            def _():
                late(k - LAG)

        q0 = pl.multiple_of(16 * j, 16)
        q = pl.ds(q0, 16)
        remote(ten.at[0, :, q], fnat.at[:, q], s_nat.at[j], r_nat.at[j], 0, 1).wait_recv()
        transform(fnat, q0, [(0, f0), (1, fp)])

    @pl.loop(NK - LAG, NK)
    def _(k):
        late(k)

    @pl.loop(0, NK)
    def _(k):
        gram(2, up_t, f0, 0, k)
        gram(5, c1b, fp, 1, k)

    routes = [
        (1, True, 0, 1),
        (2, True, 0, 1),
        (3, True, 1, 0),
        (4, True, 1, 1),
        (5, False, 0, -1),
        (5, True, 1, 1),
        (6, True, -1, 1),
    ]
    sends = []
    for i, (r, flip, dc, dy) in enumerate(routes):
        v = acc[r]
        rsend[i, :, pl.ds(0, S)] = v.T if flip else v
        cp = remote(rsend.at[i], rin.at[i], s_res.at[i], r_res.at[i], dc, dy)
        cp.start()
        sends.append(cp)

    def put(g, dy, v):
        out[g + 1, pl.ds(pl.multiple_of(rw(dy) * S, 16), S), :] = v

    put(0, 0, acc[0].T)
    put(0, 1, acc[1])
    put(1, 0, acc[3])
    put(1, 1, acc[4])
    put(-1, 1, acc[6])
    landed = [(0, -1), (0, -2), (-1, 0), (-1, -1), (1, 2), (-1, -2), (1, -1)]
    for i, (g, dy) in enumerate(landed):
        sends[i].wait_recv()
        put(g, dy, rin[i, :, pl.ds(0, S)])

    for cp in sends + occ_sends + vir_sends + nat_sends:
        cp.wait_send()

    @pl.loop(0, NK)
    def _(k):
        up_send(k).wait_send()
        c1a_send(k).wait_send()
        c1b_send(k).wait_send()
        cmb_send(k).wait_send()


def per_device(ncl, nri, tensor, live, sizes, occ, vir):
    S, B = tensor.shape[2], tensor.shape[3]
    NQ, NK = S // 16, 3 * (B // MC)
    block = pltpu.VMEM((3, B, S, B), BF)
    dma = lambda n: pltpu.SemaphoreType.DMA((n,))
    n_other = 3 * nri - 1
    any_, smem = pl.BlockSpec(memory_space=pl.ANY), pl.BlockSpec(memory_space=pltpu.SMEM)
    result = pl.pallas_call(
        functools.partial(kernel, ncl, nri),
        out_shape=jax.ShapeDtypeStruct((3, nri * S, S), F32),
        in_specs=[any_, smem, smem, any_, any_],
        out_specs=pl.BlockSpec(memory_space=pltpu.VMEM),
        scratch_shapes=[
            pltpu.VMEM((3, S, B, B), BF), pltpu.VMEM((3, S, B, B), BF),
            block, block, block, block, block,
            block, block, block, block, block,
            pltpu.VMEM((3, 16, B, 3 * B), BF),
            pltpu.VMEM((256, 256), BF),
            pltpu.VMEM((3 * B, 5 * B), BF),
            pltpu.VMEM((3, B, B), BF),
            pltpu.VMEM((3, B, B), BF),
            pltpu.VMEM((3, 3, B, B), BF),
            pltpu.VMEM((7, S, S), F32),
            pltpu.VMEM((7, S, 128), F32),
            pltpu.VMEM((7, S, 128), F32),
            dma(NQ), dma(NQ), dma(3),
            dma(NK), dma(NK), dma(NK), dma(NK), dma(NK), dma(NK), dma(NK), dma(NK),
            dma(nri - 1), dma(nri - 1), dma(n_other), dma(n_other), dma(2),
            dma(7), dma(7),
        ],
        compiler_params=pltpu.CompilerParams(
            collective_id=0, has_side_effects=True, vmem_limit_bytes=63 * 1024 * 1024
        ),
        name="polar",
    )(tensor, live, sizes, occ, vir)
    return result[None]


def solution(mesh):
    ncl, nri = mesh.shape["pair"], mesh.shape["ri"]
    in_specs = (
        P("pair", None, "ri", None, None),
        P(),
        P(),
        P("pair", None, "ri", None),
        P("pair", None, "ri", None),
    )
    return jax.shard_map(
        functools.partial(per_device, ncl, nri),
        mesh=mesh,
        in_specs=in_specs,
        out_specs=P("pair", None, None, "ri"),
        check_vma=False,
    )
```

time: 418 us -> 141 us (0.34)
  waiting for transfers between devices: 220 us -> 0 us
  Pallas kernels: 0 us -> 137 us
  local copies, waits for them, and re-layouts: 75.2 us -> 3.15 us
  matrix products: 32.9 us -> 0 us
  other arithmetic: 26.6 us -> 0 us
  blocking collectives: 24.3 us -> 0 us
  starting transfers between devices: 22.8 us -> 0 us
  between operations: 13.6 us -> 0.01 us
    pallas_call x0 -> x1, Pallas kernels: none -> 137 us  [per_device(): pl.pallas_call(functools.partial(kernel, ncl, nri), out_shape=jax.ShapeDt...]
    all_to_all x2 -> x0, waiting for transfers between devices: 135 us -> none  [the longest x1 135 us: per_device(): lax.all_to_all(near_all, 'ri', split_axis=2, concat_axis=1, tiled=True)]
    reshape x3 -> x0, local copies, waits for them, and re-layouts: 48.2 us -> none  [the longest x1 21.6 us: per_device(): near_flat = regrouped.reshape(3, 3, ri_whole, -1)]
    psum x1 -> x0, waiting for transfers between devices: 48 us -> none  [per_device(): summed = lax.psum(polar_terms, 'ri')]
    ppermute x4 -> x0, waiting for transfers between devices: 37 us -> none  [from_behind(): lax.ppermute(array, axis, [(i, (i + by) % length) for i in range(length)])]
    dot_general x17 -> x0, matrix products: 32.9 us -> none  [the longest x9 18 us: per_device(): jnp.einsum('mn,pms->pns', occ_row[1 - g], halves[u - g], preferred_elemen...]
    all_gather x2 -> x0, blocking collectives: 24.3 us -> none  [the longest x1 12.4 us: per_device(): lax.all_gather(vir_density, 'ri', axis=2, tiled=True)]
    another operation x4 -> x0, other arithmetic: 21.4 us -> none  [the longest x2 11.2 us: per_device(): jnp.stack(near_list).reshape(9, ri_share, basis_width, basis_width)]
  transfers between devices with their start and end apart: 7 -> 0, of which waited for: 4 -> 0; matrix products, arithmetic and copies ran while one was open for 17% -> 0% of each run, Pallas kernels for 0% -> 0%
where the time goes in v1:
time: 141 us; the launch traced here: 140 us
  Pallas kernels  137 us (97%)
  local copies, waits for them, and re-layouts  3.15 us (2%)
    pallas_call x1, Pallas kernels, per_device(): pl.pallas_call(functools.partial(kernel, ncl, nri), out_shape=jax.ShapeDt...  137 us

profile of v1, /device:TPU:8, one launch (start us, length us, event | category | flops | bytes accessed | tf_op | source)
XLA Modules:
  0.0 139.8 jit_solution(13976898677041303450)
XLA Ops:
  0.0 1.4 copy.6.live
  1.4 136.6 %polar.1 = f32[3,192,48]{2,1,0:T(8,128)} custom-call(bf16[1,3,48,128,128]{4,3,2,1,0:T(8,128)(2,1)} %ten.1, s32[64,3]{1,0:T(8,128)} %copy.6.live, s32[64]{0:T(128)} %sizes.1, bf16[1,3,32,128]{3,2,1,0:T(8,128)(2,1)} %occ.1, bf16[1,3,32,128]{3,2,1,0:T(8,128)(2,1)} %vir.1), custom_call_target="tpu_custom_call" | custom-call | tf_op jit(solution)/shard_map/polar/pallas_call | solution.py:291
  138.0 1.8 %copy.7 = f32[1,3,192,48]{2,3,1,0:T(8,128)} copy(f32[1,3,192,48]{3,2,1,0:T(8,128)} %bitcast.1) | data formatting | bytes 221184 | tf_op jit(solution)/shard_map/broadcast_in_dim | solution.py:319

commit v2 on v1

--- a/solution.py
+++ b/solution.py
@@ -69,28 +69,41 @@
     ).astype(BF)
     for r in range(acc.shape[0]):
         acc[r] = jnp.zeros(acc.shape[1:], F32)
+    def relay(s, mc):
+        for mb in range(MC // 16):
+            m0 = pl.multiple_of(mc * MC + mb * 16, 16)
+            for j in range(NQ):
+                x = nat[s, pl.ds(16 * j, 16), pl.ds(m0, 16), :].reshape(256, B)
+                t = jnp.dot(perm[...], x, preferred_element_type=F32).astype(BF)
+                own_t[s, pl.ds(m0, 16), pl.ds(16 * j, 16), :] = t.reshape(16, 16, B)
+
+    nat_copies[0].wait()
+
+    @pl.loop(0, NMC)
+    def _(mc):
+        relay(0, mc)
+
     pl.semaphore_wait(barrier, len(others))
 
-    occ_sends, vir_sends = [], []
+    first_sends = []
     for dy in range(1, nri):
-        occ_sends.append(
+        first_sends.append(
             remote(occ.at[0], occ_f.at[:, my_rows], s_occ.at[dy - 1], r_occ.at[dy - 1], 0, dy)
         )
-    for i, (dc, dy) in enumerate(others):
-        vir_sends.append(
-            remote(vir.at[0], vir_f.at[1 - dc, :, my_rows], s_vir.at[i], r_vir.at[i], dc, dy)
+        first_sends.append(
+            remote(vir.at[0], vir_f.at[1, :, my_rows], s_vir.at[dy - 1], r_vir.at[dy - 1], 0, dy)
         )
-    for cp in occ_sends + vir_sends:
+    for cp in first_sends:
         cp.start()
 
-    nat_sends = []
-    for j in range(NQ):
-        q = pl.ds(16 * j, 16)
-        nat_sends.append(
-            remote(ten.at[0, :, q], fnat.at[:, q], s_nat.at[j], r_nat.at[j], 0, 1)
-        )
-    for cp in nat_sends:
-        cp.start()
+    def nat_send(j):
+        n = S // NK
+        q = pl.ds(pl.multiple_of(n * j, n), n)
+        return remote(ten.at[0, :, q], fnat.at[:, q], s_nat.at[j], r_nat.at[j], 0, 1)
+
+    @pl.loop(0, NK)
+    def _(j):
+        nat_send(j).start()
 
     def part(k):
         return lax.div(k, NMC), pl.ds(pl.multiple_of(lax.rem(k, NMC) * MC, MC), MC)
@@ -111,30 +124,41 @@
         s, m = part(k)
         return remote(up_t.at[s, m], cmb.at[s, m], s_cmb.at[k], r_cmb.at[k], 1, 0)
 
-    for s in range(3):
+    @pl.loop(0, NMC)
+    def _(k):
+        up_send(k).start()
+
+    for cp in den_copies:
+        cp.wait()
+    for cp in first_sends:
+        cp.wait_recv()
+    next_sends = [
+        remote(vir_f.at[1], vir_f.at[1 - dc], s_vir.at[nri + dc], r_vir.at[nri + dc], dc, 0)
+        for dc in (-1, 1)
+    ]
+    for cp in next_sends:
+        cp.start()
+
+    @pl.loop(0, NMC)
+    def _(k):
+        c1a_send(k).start()
+
+    for s in (1, 2):
         nat_copies[s].wait()
 
         @pl.loop(0, NMC)
         def _(mc, s=s):
-            for mb in range(MC // 16):
-                m0 = pl.multiple_of(mc * MC + mb * 16, 16)
-                for j in range(NQ):
-                    x = nat[s, pl.ds(16 * j, 16), pl.ds(m0, 16), :].reshape(256, B)
-                    t = jnp.dot(perm[...], x, preferred_element_type=F32).astype(BF)
-                    own_t[s, pl.ds(m0, 16), pl.ds(16 * j, 16), :] = t.reshape(16, 16, B)
-            k = s * NMC + mc
-            up_send(k).start()
-            c1a_send(k).start()
-
-    for cp in den_copies:
-        cp.wait()
-    for cp in occ_sends + vir_sends:
+            relay(s, mc)
+            up_send(s * NMC + mc).start()
+            c1a_send(s * NMC + mc).start()
+
+    for cp in next_sends:
         cp.wait_recv()
     size = {d: sizes[cl(d)] for d in range(-2, 3)}
     ri_ = lax.broadcasted_iota(jnp.int32, (B, B), 0)
     ci_ = lax.broadcasted_iota(jnp.int32, (B, B), 1)
     for u in (-1, 0, 1):
-        on = live[c, u + 1].astype(F32)
+        on = live[u + 1, c].astype(F32)
         for t in (u - 1, u, u + 1):
             keep = jnp.where((ri_ < size[u]) & (ci_ < size[t]), on, 0.0)
             v = vir_f[u + 1, t - u + 1].astype(F32) * keep
@@ -149,8 +173,8 @@
         o = jnp.where((ri_ < size[0]) & (ci_ < size[g]), o, 0.0)
         omat[g + 1] = o.T.astype(BF)
 
-    def transform(src, q0, dests):
-        @pl.loop(0, 8)
+    def apply(src, q0, first, count, gs):
+        @pl.loop(first, first + count)
         def _(i):
             qs = [q0 + 2 * i, q0 + 2 * i + 1]
             x = jnp.concatenate(
@@ -170,16 +194,17 @@
             yy = jnp.concatenate([lo, mid, hi], axis=1)
             for n in range(2):
                 rows = yy[n * B : (n + 1) * B]
-                for slot, (g, _dst) in enumerate(dests):
+                for slot, g in enumerate(gs):
                     zn[slot, 2 * i + n] = jnp.dot(
                         omat[g + 1], rows[:, (g + 1) * B : (g + 4) * B],
                         preferred_element_type=F32,
                     ).astype(BF)
 
+    def lead(q0, dests):
         @pl.loop(0, B // 16)
         def _(mb):
             m0 = pl.multiple_of(mb * 16, 16)
-            for slot, (_g, dst) in enumerate(dests):
+            for slot, dst in enumerate(dests):
                 x = zn[slot, :, pl.ds(m0, 16), :].reshape(256, 3 * B)
                 t = jnp.dot(perm[...], x, preferred_element_type=F32).astype(BF)
                 for s in range(3):
@@ -189,96 +214,145 @@
 
     @pl.loop(0, NQ)
     def _(j):
-        transform(nat, pl.multiple_of(16 * j, 16), [(-1, zm), (0, z0), (1, zp)])
-
-    def gram(r, left, right, dc, k):
-        s, _ = part(k)
-        m0 = lax.rem(k, NMC) * MC
-        total = jnp.zeros((S, S), F32)
-        for i in range(MC // 2):
-            a = jnp.concatenate([left[s, m0 + 2 * i], left[s, m0 + 2 * i + 1]], axis=1)
-            b = jnp.concatenate([right[s, m0 + 2 * i], right[s, m0 + 2 * i + 1]], axis=1)
+        q0 = pl.multiple_of(16 * j, 16)
+        apply(nat, q0, 0, 8, (-1, 0, 1))
+        lead(q0, (zm, z0, zp))
+
+    for cp in first_sends + next_sends:
+        cp.wait_send()
+
+    def gram(r, left, right, dc, s, m0, count, lo=0, hi=None):
+        hi = S if hi is None else hi
+        total = jnp.zeros((S, hi - lo), F32)
+        for i in range(0, count, 2):
+            a = jnp.concatenate([left[s, m0 + i], left[s, m0 + i + 1]], axis=1)
+            b = jnp.concatenate(
+                [right[s, m0 + i, pl.ds(lo, hi - lo)], right[s, m0 + i + 1, pl.ds(lo, hi - lo)]],
+                axis=1,
+            )
             total += lax.dot_general(a, b, NT, preferred_element_type=F32)
-        acc[r] += total * live[cl(dc), s].astype(F32)
+        acc[r, :, pl.ds(lo, hi - lo)] += total * live[s, cl(dc)].astype(F32)
+
+    def chunk(r, left, right, dc, k):
+        gram(r, left, right, dc, lax.div(k, NMC), lax.rem(k, NMC) * MC, MC)
+
+    def halfway(r, left, right, dc, h, lo=0, hi=None):
+        gram(r, left, right, dc, lax.div(h, 2), lax.rem(h, 2) * (B // 2), B // 2, lo, hi)
 
     def late(k):
         c1b_send(k).wait_recv()
-        gram(4, c1b, zp, 1, k)
+        chunk(4, c1b, zp, 1, k)
         cmb_send(k).wait_recv()
-        gram(6, cmb, zm, -1, k)
+        chunk(6, cmb, zm, -1, k)
+        c1b_send(k).wait_send()
+        cmb_send(k).wait_send()
 
     cpj = NK // NQ
-
-    @pl.loop(0, NQ)
-    def _(j):
-        @pl.loop(0, cpj)
-        def _(kk):
-            k = j * cpj + kk
+    PQ = 8 // cpj
+    CUT = S - 16
+
+    def arrivals(first, last):
+        @pl.loop(first, last)
+        def _(k):
             up_send(k).wait_recv()
             c1b_send(k).start()
             cmb_send(k).start()
-            gram(0, own_t, z0, 0, k)
-            gram(1, up_t, z0, 0, k)
+            chunk(0, own_t, z0, 0, k)
+            chunk(1, up_t, z0, 0, k)
             c1a_send(k).wait_recv()
-            gram(3, c1a, zp, 1, k)
+            chunk(3, c1a, zp, 1, k)
+            up_send(k).wait_send()
+            c1a_send(k).wait_send()
 
             @pl.when(k >= LAG)
             def _():
                 late(k - LAG)
 
-        q0 = pl.multiple_of(16 * j, 16)
-        q = pl.ds(q0, 16)
-        remote(ten.at[0, :, q], fnat.at[:, q], s_nat.at[j], r_nat.at[j], 0, 1).wait_recv()
-        transform(fnat, q0, [(0, f0), (1, fp)])
+            q0 = pl.multiple_of(lax.div(k, cpj) * 16, 16)
+            i = lax.rem(k, cpj)
+            nat_send(k).wait_recv()
+            apply(fnat, q0, i * PQ, PQ, (0, 1))
+            nat_send(k).wait_send()
+
+            @pl.when(i == cpj - 1)
+            def _():
+                lead(q0, (f0, fp))
+
+    arrivals(0, (NQ - 1) * cpj)
+
+    EARLY = 6 * (NQ - 1) // NQ - 1
+    if CUT:
+
+        @pl.loop(0, EARLY)
+        def _(h):
+            halfway(2, up_t, f0, 0, h, 0, CUT)
+            halfway(5, c1b, fp, 1, h, 0, CUT)
+
+    arrivals((NQ - 1) * cpj, NK)
+    slots = [
+        (1, False), (2, False), (3, False), (4, False), (5, False), (5, True), (6, False)
+    ]
+    sends = []
+
+    def deliver(first, count, dc, dy):
+        for i in range(first, first + count):
+            r, flip = slots[i]
+            v = acc[r]
+            rsend[i, :, pl.ds(0, S)] = v.T if flip else v
+        run = pl.ds(first, count)
+        cp = remote(
+            rsend.at[run], rin.at[run], s_res.at[len(sends)], r_res.at[len(sends)], dc, dy
+        )
+        cp.start()
+        sends.append(cp)
+
+    deliver(0, 1, 0, 1)
+    deliver(2, 1, 1, 0)
+    @pl.loop(0, EARLY)
+    def _(h):
+        halfway(2, up_t, f0, 0, h, CUT, S)
+        halfway(5, c1b, fp, 1, h, CUT, S)
+
+    @pl.loop(EARLY, 5)
+    def _(h):
+        halfway(2, up_t, f0, 0, h)
+        halfway(5, c1b, fp, 1, h)
+
+    halfway(2, up_t, f0, 0, 5)
+    deliver(1, 1, 0, 1)
 
     @pl.loop(NK - LAG, NK)
     def _(k):
         late(k)
 
-    @pl.loop(0, NK)
-    def _(k):
-        gram(2, up_t, f0, 0, k)
-        gram(5, c1b, fp, 1, k)
-
-    routes = [
-        (1, True, 0, 1),
-        (2, True, 0, 1),
-        (3, True, 1, 0),
-        (4, True, 1, 1),
-        (5, False, 0, -1),
-        (5, True, 1, 1),
-        (6, True, -1, 1),
-    ]
-    sends = []
-    for i, (r, flip, dc, dy) in enumerate(routes):
-        v = acc[r]
-        rsend[i, :, pl.ds(0, S)] = v.T if flip else v
-        cp = remote(rsend.at[i], rin.at[i], s_res.at[i], r_res.at[i], dc, dy)
-        cp.start()
-        sends.append(cp)
-
-    def put(g, dy, v):
-        out[g + 1, pl.ds(pl.multiple_of(rw(dy) * S, 16), S), :] = v
-
-    put(0, 0, acc[0].T)
-    put(0, 1, acc[1])
-    put(1, 0, acc[3])
-    put(1, 1, acc[4])
-    put(-1, 1, acc[6])
-    landed = [(0, -1), (0, -2), (-1, 0), (-1, -1), (1, 2), (-1, -2), (1, -1)]
+    deliver(6, 1, -1, 1)
+    halfway(5, c1b, fp, 1, 5)
+    deliver(3, 2, 1, 1)
+    deliver(5, 1, 0, -1)
+
+    blocks = {
+        (0, 0): acc[0],
+        (0, 1): acc[1].T,
+        (1, 0): acc[3].T,
+        (1, 1): acc[4].T,
+        (-1, 1): acc[6].T,
+    }
+    landed = [(0, 3), (0, 2), (-1, 0), (-1, 3), (-1, 2), (1, 2), (1, 3)]
+    for cp in sends:
+        cp.wait_recv()
     for i, (g, dy) in enumerate(landed):
-        sends[i].wait_recv()
-        put(g, dy, rin[i, :, pl.ds(0, S)])
-
-    for cp in sends + occ_sends + vir_sends + nat_sends:
+        blocks[g, dy] = rin[i, :, pl.ds(0, S)]
+    for yy in range(nri):
+
+        @pl.when(y == yy)
+        def _(yy=yy):
+            for g in (-1, 0, 1):
+                out[g + 1] = jnp.concatenate(
+                    [blocks[g, (py - yy) % nri] for py in range(nri)], axis=1
+                )
+
+    for cp in sends:
         cp.wait_send()
-
-    @pl.loop(0, NK)
-    def _(k):
-        up_send(k).wait_send()
-        c1a_send(k).wait_send()
-        c1b_send(k).wait_send()
-        cmb_send(k).wait_send()
 
 
 def per_device(ncl, nri, tensor, live, sizes, occ, vir):
@@ -286,11 +360,11 @@
     NQ, NK = S // 16, 3 * (B // MC)
     block = pltpu.VMEM((3, B, S, B), BF)
     dma = lambda n: pltpu.SemaphoreType.DMA((n,))
-    n_other = 3 * nri - 1
+    n_vir = nri + 2
     any_, smem = pl.BlockSpec(memory_space=pl.ANY), pl.BlockSpec(memory_space=pltpu.SMEM)
     result = pl.pallas_call(
         functools.partial(kernel, ncl, nri),
-        out_shape=jax.ShapeDtypeStruct((3, nri * S, S), F32),
+        out_shape=jax.ShapeDtypeStruct((3, S, nri * S), F32),
         in_specs=[any_, smem, smem, any_, any_],
         out_specs=pl.BlockSpec(memory_space=pltpu.VMEM),
         scratch_shapes=[
@@ -306,17 +380,17 @@
             pltpu.VMEM((7, S, S), F32),
             pltpu.VMEM((7, S, 128), F32),
             pltpu.VMEM((7, S, 128), F32),
-            dma(NQ), dma(NQ), dma(3),
+            dma(NK), dma(NK), dma(3),
             dma(NK), dma(NK), dma(NK), dma(NK), dma(NK), dma(NK), dma(NK), dma(NK),
-            dma(nri - 1), dma(nri - 1), dma(n_other), dma(n_other), dma(2),
-            dma(7), dma(7),
+            dma(nri - 1), dma(nri - 1), dma(n_vir), dma(n_vir), dma(2),
+            dma(6), dma(6),
         ],
         compiler_params=pltpu.CompilerParams(
             collective_id=0, has_side_effects=True, vmem_limit_bytes=63 * 1024 * 1024
         ),
         name="polar",
-    )(tensor, live, sizes, occ, vir)
-    return result[None]
+    )(tensor, live.T, sizes, occ, vir)
+    return jnp.swapaxes(result, 1, 2)[None]
 
 
 def solution(mesh):

time: 141 us -> 132 us (0.936)
  Pallas kernels: 137 us -> 130 us
  local copies, waits for them, and re-layouts: 3.15 us -> 1.58 us
    pallas_call x1, Pallas kernels: 137 us -> 130 us  [per_device(): pl.pallas_call(functools.partial(kernel, ncl, nri), out_shape=jax.ShapeDt...]
    broadcast_in_dim x1 -> x0, local copies, waits for them, and re-layouts: 1.77 us -> none  [per_device(): return result[None]]
where the time goes in v2:
time: 132 us
  Pallas kernels  130 us (98%)
  local copies, waits for them, and re-layouts  1.58 us (1%)
    pallas_call x1, Pallas kernels, per_device(): pl.pallas_call(functools.partial(kernel, ncl, nri), out_shape=jax.ShapeDt...  130 us

profile of v2, /device:TPU:8, one launch (start us, length us, event | category | flops | bytes accessed | tf_op | source)
XLA Modules:
  0.0 131.5 jit_solution(351225432217457828)
XLA Ops:
  0.0 129.9 %polar.1 = f32[3,48,192]{2,1,0:T(8,128)} custom-call(bf16[1,3,48,128,128]{4,3,2,1,0:T(8,128)(2,1)} %ten.1, s32[3,64]{1,0:T(4,128)} %bitcast.5, s32[64]{0:T(128)} %sizes.1, bf16[1,3,32,128]{3,2,1,0:T(8,128)(2,1)} %occ.1, bf16[1,3,32,128]{3,2,1,0:T(8,128)(2,1)} %vir.1), custom_call_target="tpu_custom_call" | custom-call | tf_op jit(solution)/shard_map/polar/pallas_call | solution.py:365
  129.9 1.6 %copy.7 = f32[1,3,192,48]{2,3,1,0:T(8,128)} copy(f32[1,3,192,48]{2,3,1,0:T(8,128)} %bitcast.4) | data formatting | bytes 221184

commit v3 on v2

--- a/solution.py
+++ b/solution.py
@@ -12,7 +12,7 @@
 F32 = jnp.float32
 NT = (((1,), (1,)), ((), ()))
 MC = 32
-LAG = 2
+SUB = 4
 
 
 def kernel(
@@ -46,7 +46,12 @@
         )
 
     barrier = pltpu.get_barrier_semaphore()
-    others = [(dc, dy) for dc in (-1, 0, 1) for dy in range(nri) if (dc, dy) != (0, 0)]
+    others = [
+        (dc, dy)
+        for dc in (-1, 0, 1)
+        for dy in range(nri)
+        if (dc, dy) != (0, 0) and (dc == 0 or dy in (0, 1, nri - 1))
+    ]
     for dc, dy in others:
         pl.semaphore_signal(barrier, inc=1, device_id=(cl(dc), rw(dy)), device_id_type=MESH)
 
@@ -105,7 +110,12 @@
     def _(j):
         nat_send(j).start()
 
+    LAST = NK - 1
+
     def part(k):
+        if isinstance(k, int) and k >= LAST:
+            n = MC // SUB
+            return 2, pl.ds(B - MC + (k - LAST) * n, n)
         return lax.div(k, NMC), pl.ds(pl.multiple_of(lax.rem(k, NMC) * MC, MC), MC)
 
     def up_send(k):
@@ -149,8 +159,16 @@
         @pl.loop(0, NMC)
         def _(mc, s=s):
             relay(s, mc)
-            up_send(s * NMC + mc).start()
-            c1a_send(s * NMC + mc).start()
+            k = s * NMC + mc
+
+            @pl.when(k < LAST)
+            def _():
+                up_send(k).start()
+                c1a_send(k).start()
+
+    for i in range(SUB):
+        up_send(LAST + i).start()
+        c1a_send(LAST + i).start()
 
     for cp in next_sends:
         cp.wait_recv()
@@ -221,74 +239,75 @@
     for cp in first_sends + next_sends:
         cp.wait_send()
 
-    def gram(r, left, right, dc, s, m0, count, lo=0, hi=None):
-        hi = S if hi is None else hi
-        total = jnp.zeros((S, hi - lo), F32)
+    def gram(r, left, right, dc, s, m0, count):
+        total = jnp.zeros((S, S), F32)
         for i in range(0, count, 2):
             a = jnp.concatenate([left[s, m0 + i], left[s, m0 + i + 1]], axis=1)
-            b = jnp.concatenate(
-                [right[s, m0 + i, pl.ds(lo, hi - lo)], right[s, m0 + i + 1, pl.ds(lo, hi - lo)]],
-                axis=1,
-            )
+            b = jnp.concatenate([right[s, m0 + i], right[s, m0 + i + 1]], axis=1)
             total += lax.dot_general(a, b, NT, preferred_element_type=F32)
-        acc[r, :, pl.ds(lo, hi - lo)] += total * live[s, cl(dc)].astype(F32)
+        acc[r] += total * live[s, cl(dc)].astype(F32)
 
     def chunk(r, left, right, dc, k):
         gram(r, left, right, dc, lax.div(k, NMC), lax.rem(k, NMC) * MC, MC)
 
-    def halfway(r, left, right, dc, h, lo=0, hi=None):
-        gram(r, left, right, dc, lax.div(h, 2), lax.rem(h, 2) * (B // 2), B // 2, lo, hi)
+    def halfway(r, left, right, dc, h):
+        gram(r, left, right, dc, lax.div(h, 2), lax.rem(h, 2) * (B // 2), B // 2)
 
     def late(k):
         c1b_send(k).wait_recv()
+        cmb_send(k).wait_recv()
         chunk(4, c1b, zp, 1, k)
-        cmb_send(k).wait_recv()
         chunk(6, cmb, zm, -1, k)
         c1b_send(k).wait_send()
         cmb_send(k).wait_send()
 
+    FROM = LAST - 4
     cpj = NK // NQ
     PQ = 8 // cpj
-    CUT = S - 16
-
-    def arrivals(first, last):
-        @pl.loop(first, last)
-        def _(k):
-            up_send(k).wait_recv()
-            c1b_send(k).start()
-            cmb_send(k).start()
-            chunk(0, own_t, z0, 0, k)
-            chunk(1, up_t, z0, 0, k)
-            c1a_send(k).wait_recv()
-            chunk(3, c1a, zp, 1, k)
-            up_send(k).wait_send()
-            c1a_send(k).wait_send()
-
-            @pl.when(k >= LAG)
-            def _():
-                late(k - LAG)
-
-            q0 = pl.multiple_of(lax.div(k, cpj) * 16, 16)
-            i = lax.rem(k, cpj)
-            nat_send(k).wait_recv()
-            apply(fnat, q0, i * PQ, PQ, (0, 1))
-            nat_send(k).wait_send()
-
-            @pl.when(i == cpj - 1)
-            def _():
-                lead(q0, (f0, fp))
-
-    arrivals(0, (NQ - 1) * cpj)
-
-    EARLY = 6 * (NQ - 1) // NQ - 1
-    if CUT:
-
-        @pl.loop(0, EARLY)
-        def _(h):
-            halfway(2, up_t, f0, 0, h, 0, CUT)
-            halfway(5, c1b, fp, 1, h, 0, CUT)
-
-    arrivals((NQ - 1) * cpj, NK)
+
+    def piece(k):
+        q0 = pl.multiple_of(lax.div(k, cpj) * 16, 16)
+        i = lax.rem(k, cpj)
+        nat_send(k).wait_recv()
+        apply(fnat, q0, i * PQ, PQ, (0, 1))
+
+        @pl.when(i == cpj - 1)
+        def _():
+            lead(q0, (f0, fp))
+
+        nat_send(k).wait_send()
+
+    @pl.loop(0, LAST)
+    def _(k):
+        c1a_send(k).wait_recv()
+        chunk(3, c1a, zp, 1, k)
+        c1a_send(k).wait_send()
+
+        @pl.when(k >= FROM)
+        def _():
+            late(2 * (k - FROM))
+            late(2 * (k - FROM) + 1)
+
+        up_send(k).wait_recv()
+        c1b_send(k).start()
+        cmb_send(k).start()
+        chunk(0, own_t, z0, 0, k)
+        chunk(1, up_t, z0, 0, k)
+        up_send(k).wait_send()
+        piece(k)
+
+    for i in range(SUB):
+        c1a_send(LAST + i).wait_recv()
+    chunk(3, c1a, zp, 1, LAST)
+    chunk(0, own_t, z0, 0, LAST)
+    late(LAST - 3)
+    late(LAST - 2)
+    for i in range(SUB):
+        up_send(LAST + i).wait_recv()
+        c1b_send(LAST + i).start()
+        cmb_send(LAST + i).start()
+    chunk(1, up_t, z0, 0, LAST)
+
     slots = [
         (1, False), (2, False), (3, False), (4, False), (5, False), (5, True), (6, False)
     ]
@@ -306,29 +325,34 @@
         cp.start()
         sends.append(cp)
 
+    deliver(2, 1, 1, 0)
     deliver(0, 1, 0, 1)
-    deliver(2, 1, 1, 0)
-    @pl.loop(0, EARLY)
-    def _(h):
-        halfway(2, up_t, f0, 0, h, CUT, S)
-        halfway(5, c1b, fp, 1, h, CUT, S)
-
-    @pl.loop(EARLY, 5)
+    piece(LAST)
+
+    @pl.loop(0, 5)
     def _(h):
         halfway(2, up_t, f0, 0, h)
         halfway(5, c1b, fp, 1, h)
 
     halfway(2, up_t, f0, 0, 5)
     deliver(1, 1, 0, 1)
-
-    @pl.loop(NK - LAG, NK)
-    def _(k):
-        late(k)
-
+    late(LAST - 1)
+    for i in range(SUB):
+        cmb_send(LAST + i).wait_recv()
+    chunk(6, cmb, zm, -1, LAST)
     deliver(6, 1, -1, 1)
+    for i in range(SUB):
+        c1b_send(LAST + i).wait_recv()
+    chunk(4, c1b, zp, 1, LAST)
+    deliver(3, 1, 1, 1)
     halfway(5, c1b, fp, 1, 5)
-    deliver(3, 2, 1, 1)
+    deliver(4, 1, 1, 1)
     deliver(5, 1, 0, -1)
+    for i in range(SUB):
+        up_send(LAST + i).wait_send()
+        c1a_send(LAST + i).wait_send()
+        c1b_send(LAST + i).wait_send()
+        cmb_send(LAST + i).wait_send()
 
     blocks = {
         (0, 0): acc[0],
@@ -381,9 +405,9 @@
             pltpu.VMEM((7, S, 128), F32),
             pltpu.VMEM((7, S, 128), F32),
             dma(NK), dma(NK), dma(3),
-            dma(NK), dma(NK), dma(NK), dma(NK), dma(NK), dma(NK), dma(NK), dma(NK),
+            *[dma(NK - 1 + SUB) for _ in range(8)],
             dma(nri - 1), dma(nri - 1), dma(n_vir), dma(n_vir), dma(2),
-            dma(6), dma(6),
+            dma(7), dma(7),
         ],
         compiler_params=pltpu.CompilerParams(
             collective_id=0, has_side_effects=True, vmem_limit_bytes=63 * 1024 * 1024

time: 132 us -> 131 us (level)
  no operation moved by 1% of the time
where the time goes in v3:
time: 131 us
  Pallas kernels  130 us (99%)
  local copies, waits for them, and re-layouts  1.58 us (1%)
    pallas_call x1, Pallas kernels, per_device(): pl.pallas_call(functools.partial(kernel, ncl, nri), out_shape=jax.ShapeDt...  130 us

profile of v3, /device:TPU:8, one launch (start us, length us, event | category | flops | bytes accessed | tf_op | source)
XLA Modules:
  0.0 131.4 jit_solution(14393481801824489155)
XLA Ops:
  0.0 129.8 %polar.1 = f32[3,48,192]{2,1,0:T(8,128)} custom-call(bf16[1,3,48,128,128]{4,3,2,1,0:T(8,128)(2,1)} %ten.1, s32[3,64]{1,0:T(4,128)} %bitcast.5, s32[64]{0:T(128)} %sizes.1, bf16[1,3,32,128]{3,2,1,0:T(8,128)(2,1)} %occ.1, bf16[1,3,32,128]{3,2,1,0:T(8,128)(2,1)} %vir.1), custom_call_target="tpu_custom_call" | custom-call | tf_op jit(solution)/shard_map/polar/pallas_call | solution.py:389
  129.8 1.6 %copy.7 = f32[1,3,192,48]{2,3,1,0:T(8,128)} copy(f32[1,3,192,48]{2,3,1,0:T(8,128)} %bitcast.4) | data formatting | bytes 221184

commit v4 on v3

--- a/solution.py
+++ b/solution.py
@@ -12,7 +12,7 @@
 F32 = jnp.float32
 NT = (((1,), (1,)), ((), ()))
 MC = 32
-SUB = 4
+SUB = 2
 
 
 def kernel(

time: 131 us -> 131 us (level)
  no operation moved by 1% of the time
where the time goes in v4:
time: 131 us
  Pallas kernels  130 us (99%)
  local copies, waits for them, and re-layouts  1.58 us (1%)
    pallas_call x1, Pallas kernels, per_device(): pl.pallas_call(functools.partial(kernel, ncl, nri), out_shape=jax.ShapeDt...  130 us

profile of v4, /device:TPU:8, one launch (start us, length us, event | category | flops | bytes accessed | tf_op | source)
XLA Modules:
  0.0 131.2 jit_solution(7199173861354302062)
XLA Ops:
  0.0 129.6 %polar.1 = f32[3,48,192]{2,1,0:T(8,128)} custom-call(bf16[1,3,48,128,128]{4,3,2,1,0:T(8,128)(2,1)} %ten.1, s32[3,64]{1,0:T(4,128)} %bitcast.5, s32[64]{0:T(128)} %sizes.1, bf16[1,3,32,128]{3,2,1,0:T(8,128)(2,1)} %occ.1, bf16[1,3,32,128]{3,2,1,0:T(8,128)(2,1)} %vir.1), custom_call_target="tpu_custom_call" | custom-call | tf_op jit(solution)/shard_map/polar/pallas_call | solution.py:389
  129.6 1.6 %copy.7 = f32[1,3,192,48]{2,3,1,0:T(8,128)} copy(f32[1,3,192,48]{2,3,1,0:T(8,128)} %bitcast.4) | data formatting | bytes 221184
